TPU v7x, 32 devices: a whole 2x2x4 slice. The times are simulated.
32 devices in a mesh: dp: 4 (over y, x), gz: 8 (over z, core).
Axes of the slice: x: 2, y: 2, z: 4, core: 2. Of those that a mesh axis runs over, the one named last changes fastest.
Arguments:
- volume: bfloat16 [8, 4, 16, 2048], P('gz', 'dp'), may hold values from -6 to 6
- weight: bfloat16 [1728, 64], replicated, may hold values from -0.15625 to 0.15625
- cotangent: bfloat16 [8, 4, 16, 2048], P('gz', 'dp'), may hold values from -6 to 6
Outputs:
- activation: bfloat16 [8, 4, 16, 2048], P('gz', 'dp')
- input_grad: bfloat16 [8, 4, 16, 2048], P('gz', 'dp')
- weight_grad: float32 [1728, 64], P('gz', 'dp')
All inputs are finite; a program needn't handle non-finite values.
Results may differ from a plain program's by a relative error of at most 0.01.
Values may be sent and summed in bfloat16 or wider, within the bound.
A program may use at most 64 MiB of HBM per device.

v0:
```python
import functools
import math

import jax
import jax.numpy as jnp
from jax import lax
from jax.experimental import pallas as pl
from jax.experimental.pallas import tpu as pltpu
from jax.sharding import PartitionSpec as P

MESH = pl.DeviceIdType.MESH
BF16 = jnp.bfloat16
F32 = jnp.float32


def rolled(x, shift, axis):
    return pltpu.roll(x, shift % x.shape[axis], axis)


def pair_rows(plane, height, pairs):
    return jnp.concatenate([plane[:, 128 * k : 128 * (k + 1)] for k in range(pairs)], axis=0)


def windows(plane, height, pairs):
    own = pair_rows(plane, height, pairs)
    zero = jnp.zeros((height, 128), own.dtype)
    after = jnp.concatenate([own[height:], zero], axis=0)
    before = jnp.concatenate([zero, own[:-height]], axis=0)
    lane = lax.broadcasted_iota(jnp.int32, own.shape, 1)
    return own, jnp.where(lane < 64, after, before)


def y_sum(parts, height):
    row = lax.broadcasted_iota(jnp.int32, (parts.shape[0], 128), 0) % height
    low = jnp.where(row == 0, 0.0, rolled(parts[:, 0:128], 1, 0))
    high = jnp.where(row == height - 1, 0.0, rolled(parts[:, 256:384], -1, 0))
    return parts[:, 128:256] + low + high


def kernel(
    geom, v_ref, w_ref, g_ref, act_ref, ig_ref, wg_ref,
    vbuf, gbuf, wbuf, dbuf, win, dwin, wfwd, wbwd,
    pack0, recv0, sum0, recv1, sum1, recv2,
    local_sem, vsend, vrecv, dsend, drecv, ssend0, srecv0, ssend1, srecv1, ssend2, srecv2,
):
    n, m, height, pairs, rows_out, cols_out, wide, scale = geom
    me = lax.axis_index("dp")
    my = lax.axis_index("gz")
    mz = m // 2
    z, core = lax.div(my, 2), lax.rem(my, 2)
    partner = my + 1 - 2 * core
    z_peers = [2 * lax.rem(z + k, mz) + core for k in range(1, mz)]

    barrier = pltpu.get_barrier_semaphore()
    for k in range(1, n):
        pl.semaphore_signal(
            barrier, inc=1, device_id={"dp": lax.rem(me + k, n)}, device_id_type=MESH
        )
    for peer in [partner] + z_peers:
        pl.semaphore_signal(barrier, inc=1, device_id={"gz": peer}, device_id_type=MESH)
    load_w = pltpu.make_async_copy(w_ref, wbuf, local_sem.at[0])
    load_v = pltpu.make_async_copy(v_ref.at[0, 0], vbuf.at[1], local_sem.at[1])
    load_g = pltpu.make_async_copy(g_ref.at[0, 0], gbuf, local_sem.at[2])
    load_w.start()
    load_v.start()
    load_g.start()
    pl.semaphore_wait(barrier, n + mz - 1)

    def halo(source, buf, ssem, rsem):
        up = pltpu.make_async_remote_copy(
            src_ref=source, dst_ref=buf.at[0], send_sem=ssem.at[0], recv_sem=rsem.at[0],
            device_id={"dp": lax.rem(me + 1, n)}, device_id_type=MESH,
        )
        down = pltpu.make_async_remote_copy(
            src_ref=source, dst_ref=buf.at[2], send_sem=ssem.at[1], recv_sem=rsem.at[1],
            device_id={"dp": lax.rem(me + n - 1, n)}, device_id_type=MESH,
        )

        @pl.when(me < n - 1)
        def _():
            up.start()

        @pl.when(me > 0)
        def _():
            down.start()

        return up, down

    def halo_arrive(up, down, buf):
        @pl.when(me > 0)
        def _():
            up.wait_recv()

        @pl.when(me == 0)
        def _():
            buf[0] = jnp.zeros(buf.shape[1:], buf.dtype)

        @pl.when(me < n - 1)
        def _():
            down.wait_recv()

        @pl.when(me == n - 1)
        def _():
            buf[2] = jnp.zeros(buf.shape[1:], buf.dtype)

    def halo_sent(up, down):
        @pl.when(me < n - 1)
        def _():
            up.wait_send()

        @pl.when(me > 0)
        def _():
            down.wait_send()

    v_up, v_down = halo(v_ref.at[0, 0], vbuf, vsend, vrecv)

    load_w.wait()
    zero = jnp.zeros((64, 64), BF16)
    for a in range(3):
        for b in range(3):
            base = (a * 9 + b * 3) * 64
            k0, k1, k2 = (wbuf[:, base + 64 * c : base + 64 * (c + 1)] for c in range(3))
            top = jnp.concatenate([k1, k2, zero, k0], axis=1)
            bottom = jnp.concatenate([k0, k1, k2, zero], axis=1)
            wfwd[128 * b : 128 * (b + 1), 256 * a : 256 * (a + 1)] = jnp.concatenate(
                [top, bottom], axis=0
            )
            left = jnp.concatenate([k1, k0, zero, k2], axis=0)
            right = jnp.concatenate([k2, k1, k0, zero], axis=0)
            fa, fb = 2 - a, 2 - b
            wbwd[256 * fa : 256 * (fa + 1), 128 * fb : 128 * (fb + 1)] = jnp.concatenate(
                [left, right], axis=1
            )

    def fill(target, buf, a):
        own, edge = windows(buf[a], height, pairs)
        target[:, 256 * a : 256 * a + 128] = own
        target[:, 256 * a + 128 : 256 * (a + 1)] = edge

    def plane_fwd(a):
        return lax.dot_general(
            win[:, 256 * a : 256 * (a + 1)], wfwd[:, 256 * a : 256 * (a + 1)],
            (((1,), (1,)), ((), ())), preferred_element_type=F32,
        )

    load_v.wait()
    fill(win, vbuf, 1)
    parts = plane_fwd(1)
    load_g.wait()
    halo_arrive(v_up, v_down, vbuf)
    fill(win, vbuf, 0)
    fill(win, vbuf, 2)
    parts = parts + plane_fwd(0) + plane_fwd(2)
    pre = y_sum(parts, height)
    sig = 1.0 / (1.0 + jnp.exp(-pre))
    cot = pair_rows(gbuf[...], height, pairs).astype(F32)
    delta = (cot * sig * (1.0 + pre * (1.0 - sig))).astype(BF16)
    for k in range(pairs):
        dbuf[1, :, 128 * k : 128 * (k + 1)] = delta[height * k : height * (k + 1)]

    d_up, d_down = halo(dbuf.at[1], dbuf, dsend, drecv)

    wide_delta = delta.astype(F32)
    row = lax.broadcasted_iota(jnp.int32, wide_delta.shape, 0) % height
    ahead = jnp.where(row == height - 1, 0.0, rolled(wide_delta, -1, 0)).astype(BF16)
    behind = jnp.where(row == 0, 0.0, rolled(wide_delta, 1, 0)).astype(BF16)
    moved = jnp.concatenate([ahead, delta, behind], axis=1)
    lane = lax.broadcasted_iota(jnp.int32, (64, 128), 1) < 64
    early = sum(2 * (q + 1) * rows_out <= 9 * 128 for q in range(mz))
    parts_z = ((0, early), (early, mz))
    zero_copies = []
    gathered = []
    lanes = lax.broadcasted_iota(jnp.int32, (64, 128), 1)

    def weight_terms(planes, low_z, high_z, stage):
        span = win[:, 256 * planes[0] : 256 * (planes[-1] + 1)]
        terms = lax.dot_general(
            moved, span, (((0,), (0,)), ((), ())), preferred_element_type=F32
        )
        quads = []
        for p in range(len(planes)):
            for b in range(3):
                first = terms[128 * b : 128 * b + 64, 256 * p : 256 * (p + 1)]
                second = terms[128 * b + 64 : 128 * (b + 1), 256 * p : 256 * (p + 1)]
                quads.append((first[:, :128], first[:, 128:], second[:, :128], second[:, 128:]))
        out_tiles = []
        for q in range(0, len(quads), 2):
            a1, a2, b1, b2 = quads[q]
            out_tiles.append(rolled(jnp.where(lane, a1, a2), 64, 1) + b1)
            third = rolled(a1, 64, 1) + b2
            if q + 1 == len(quads):
                out_tiles.append(jnp.where(lane, third, 0.0))
                continue
            c1, c2, e1, e2 = quads[q + 1]
            out_tiles.append(jnp.where(lane, third, c2 + rolled(e1, 64, 1)))
            out_tiles.append(c1 + rolled(jnp.where(lane, e2, e1), 64, 1))
        gathered.extend(tile * scale for tile in out_tiles)
        for g in range(2 * low_z, 2 * high_z):
            start, offset = (g * rows_out) // 128, (g * rows_out) % 128
            for j in range(wide):
                tile = gathered[start + j]
                if offset:
                    tile = rolled(tile, -offset, 1)
                    if (g + 1) * rows_out > 128 * (start + j + 1):
                        after = rolled(gathered[start + j + 1], -offset, 1)
                        tile = jnp.where(lanes < 128 - offset, tile, after)
                tile = tile.astype(BF16)
                for d in range(n):
                    part = tile[cols_out * d : cols_out * (d + 1)]
                    if cols_out % 16:
                        fill_rows = jnp.zeros((pack0.shape[4] - cols_out, 128), BF16)
                        part = jnp.concatenate([part, fill_rows], axis=0)
                    pack0[g % 2, g // 2, d, j] = part
        copy = pltpu.make_async_remote_copy(
            src_ref=pack0.at[1 - core, low_z:high_z], dst_ref=recv0.at[low_z:high_z],
            send_sem=ssend0.at[stage], recv_sem=srecv0.at[stage],
            device_id={"gz": partner}, device_id_type=MESH,
        )
        copy.start()
        zero_copies.append(copy)

    weight_terms((0, 1), 0, early, 0)
    weight_terms((2,), early, mz, 1)

    act = (pre * sig).astype(BF16)
    for k in range(pairs):
        act_ref[0, 0, :, 128 * k : 128 * (k + 1)] = act[height * k : height * (k + 1)]

    first_copies = []
    for stage, (low_z, high_z) in enumerate(parts_z):
        zero_copies[stage].wait_recv()
        both = pack0[core, low_z:high_z].astype(F32) + recv0[low_z:high_z].astype(F32)
        sum0[low_z:high_z] = both.astype(BF16)
        copies = []
        for k in range(1, n):
            peer = lax.rem(me + k, n)
            copy = pltpu.make_async_remote_copy(
                src_ref=sum0.at[low_z:high_z, peer], dst_ref=recv1.at[k - 1, low_z:high_z],
                send_sem=ssend1.at[stage, k - 1], recv_sem=srecv1.at[stage, k - 1],
                device_id={"dp": peer}, device_id_type=MESH,
            )
            copy.start()
            copies.append(copy)
        first_copies.append(copies)

    halo_arrive(d_up, d_down, dbuf)
    for a in range(3):
        fill(dwin, dbuf, a)
    back = jnp.dot(dwin[...], wbwd[...], preferred_element_type=F32)
    grad = y_sum(back, height).astype(BF16)
    for k in range(pairs):
        ig_ref[0, 0, :, 128 * k : 128 * (k + 1)] = grad[height * k : height * (k + 1)]

    second_copies = []
    for k in range(1, mz):
        second_copies.append(pltpu.make_async_remote_copy(
            src_ref=sum1.at[lax.rem(z + k, mz)], dst_ref=recv2.at[k - 1],
            send_sem=ssend2.at[k - 1], recv_sem=srecv2.at[k - 1],
            device_id={"gz": z_peers[k - 1]}, device_id_type=MESH,
        ))
    for stage, (low_z, high_z) in enumerate(parts_z):
        total = sum0[low_z:high_z, me].astype(F32)
        for k in range(1, n):
            first_copies[stage][k - 1].wait_recv()
            total = total + recv1[k - 1, low_z:high_z].astype(F32)
        sum1[low_z:high_z] = total.astype(BF16)
        for k in range(1, mz):
            target = lax.rem(z + k, mz)

            @pl.when((target < early) if stage == 0 else (target >= early))
            def _(copy=second_copies[k - 1]):
                copy.start()

    halo_sent(v_up, v_down)
    halo_sent(d_up, d_down)
    for copy in zero_copies + first_copies[0] + first_copies[1]:
        copy.wait_send()
    total = sum1[z].astype(F32)
    for k in range(1, mz):
        second_copies[k - 1].wait_recv()
        total = total + recv2[k - 1].astype(F32)
    for t in range(wide):
        count = min(128, rows_out - 128 * t)
        wg_ref[:, 128 * t : 128 * t + count] = total[t, :cols_out, :count]
    for copy in second_copies:
        copy.wait_send()


def place(a_ref, i_ref, w_ref, act_ref, ig_ref, wg_ref, sem):
    pairs = ((a_ref, act_ref), (i_ref, ig_ref), (w_ref, wg_ref))
    copies = [pltpu.make_async_copy(a, b, sem.at[k]) for k, (a, b) in enumerate(pairs)]
    for copy in copies:
        copy.start()
    for copy in copies:
        copy.wait()


def per_device(volume, weight, cotangent):
    n = lax.axis_size("dp")
    m = lax.axis_size("gz")
    chans = weight.shape[1]
    universes, planes, height, merged = volume.shape
    assert chans == 64 and universes == 1 and planes == 1
    pairs = merged // 128
    cells = height * pairs * 2
    rows_out = weight.shape[0] // m
    cols_out = chans // n
    padded = -(-cols_out // 16) * 16
    wide = -(-rows_out // 128)
    assert 27 * 64 == weight.shape[0]
    scale = 1.0 / math.sqrt(n * m * cells)
    geom = (n, m, height, pairs, rows_out, cols_out, wide, scale)
    vmem = pltpu.VMEM
    dma = pltpu.SemaphoreType.DMA
    block = (height, merged)
    grid_rows = pairs * height
    results = pl.pallas_call(
        functools.partial(kernel, geom),
        out_shape=(
            vmem(volume.shape, BF16),
            vmem(volume.shape, BF16),
            vmem((cols_out, rows_out), F32),
        ),
        in_specs=[pl.BlockSpec(memory_space=pltpu.HBM)] * 3,
        out_specs=[pl.BlockSpec(memory_space=pltpu.VMEM)] * 3,
        scratch_shapes=[
            vmem((3, *block), BF16),
            vmem(block, BF16),
            vmem(weight.shape[::-1], BF16),
            vmem((3, *block), BF16),
            vmem((grid_rows, 768), BF16),
            vmem((grid_rows, 768), BF16),
            vmem((384, 768), BF16),
            vmem((768, 384), BF16),
            vmem((2, m // 2, n, wide, padded, 128), BF16),
            vmem((m // 2, n, wide, padded, 128), BF16),
            vmem((m // 2, n, wide, padded, 128), BF16),
            vmem((n - 1, m // 2, wide, padded, 128), BF16),
            vmem((m // 2, wide, padded, 128), BF16),
            vmem((m // 2 - 1, wide, padded, 128), BF16),
            dma((3,)), dma((2,)), dma((2,)), dma((2,)), dma((2,)),
            dma((2,)), dma((2,)), dma((2, n - 1)), dma((2, n - 1)),
            dma((m // 2 - 1,)), dma((m // 2 - 1,)),
        ],
        compiler_params=pltpu.CompilerParams(
            collective_id=0, has_side_effects=True, vmem_limit_bytes=32 * 1024 * 1024
        ),
    )(*(pltpu.with_memory_space_constraint(x, pltpu.HBM) for x in (volume, weight.T, cotangent)))
    activation, input_grad, weight_grad = pl.pallas_call(
        place,
        out_shape=tuple(jax.ShapeDtypeStruct(r.shape, r.dtype) for r in results),
        in_specs=[pl.BlockSpec(memory_space=pl.ANY)] * 3,
        out_specs=[pl.BlockSpec(memory_space=pl.ANY)] * 3,
        scratch_shapes=[dma((3,))],
        compiler_params=pltpu.CompilerParams(vmem_limit_bytes=1024 * 1024),
    )(*results)
    return activation, input_grad, weight_grad.T


def solution(mesh):
    return jax.shard_map(
        per_device,
        mesh=mesh,
        in_specs=(P("gz", "dp", None, None), P(), P("gz", "dp", None, None)),
        out_specs=(P("gz", "dp", None, None), P("gz", "dp", None, None), P("gz", "dp")),
        check_vma=False,
    )
```

profile of v0, /device:TPU:0, one launch (start us, length us, event | category | flops | bytes accessed | tf_op | source)
XLA Modules:
  0.0 20.7 jit_solution(10477651644255531126)
XLA Ops:
  0.6 19.4 %shard_map.58 = (bf16[1,1,16,2048]{3,2,1,0:T(8,128)(2,1)S(1)}, bf16[1,1,16,2048]{3,2,1,0:T(8,128)(2,1)S(1)}, f32[16,216]{1,0:T(8,128)S(1)}) custom-call(bf16[1,1,16,2048]{3,2,1,0:T(8,128)(2,1)} %v_ref.1, bf16[64,1728]{1,0:T(8,128)(2,1)} %bitcast.2, bf16[1,1,16,2048]{3,2,1,0:T(8,128)(2,1)} %g_ref.1), custom_call_target="tpu_custom_call" | custom-call | tf_op jit(solution)/shard_map/pallas_call | solution.py:317
  20.0 0.7 %shard_map.59 = (bf16[1,1,16,2048]{3,2,1,0:T(8,128)(2,1)}, bf16[1,1,16,2048]{3,2,1,0:T(8,128)(2,1)}, f32[16,216]{1,0:T(8,128)}) custom-call(bf16[1,1,16,2048]{3,2,1,0:T(8,128)(2,1)S(1)} %get-tuple-element.9.a_ref, bf16[1,1,16,2048]{3,2,1,0:T(8,128)(2,1)S(1)} %get-tuple-element.10.i_ref, f32[16,216]{1,0:T(8,128)S(1)} %get-tuple-element.11.w_ref), custom_call_target="tpu_custom_call" | custom-call | tf_op jit(solution)/shard_map/pallas_call | solution.py:349
where the time goes:
time: 20.9 us; the launch traced here: 20.7 us
  Pallas kernels  20.1 us (96%)
  between operations  0.64 us (3%)
    pallas_call x1, Pallas kernels, per_device(): pl.pallas_call(functools.partial(kernel, geom), out_shape=(vmem(volume.sh...  19.4 us
    pallas_call x1, Pallas kernels, per_device(): pl.pallas_call(place, out_shape=tuple((jax.ShapeDtypeStruct(r.shape, r.dt...  0.68 us

commit v1 on v0

--- a/solution.py
+++ b/solution.py
@@ -86,7 +86,7 @@
 
         return up, down
 
-    def halo_arrive(up, down, buf):
+    def arrive_low(up, buf):
         @pl.when(me > 0)
         def _():
             up.wait_recv()
@@ -95,6 +95,7 @@
         def _():
             buf[0] = jnp.zeros(buf.shape[1:], buf.dtype)
 
+    def arrive_high(down, buf):
         @pl.when(me < n - 1)
         def _():
             down.wait_recv()
@@ -102,6 +103,27 @@
         @pl.when(me == n - 1)
         def _():
             buf[2] = jnp.zeros(buf.shape[1:], buf.dtype)
+
+    lower = me < n // 2
+    near = jnp.where(lower, 0, 2)
+
+    def halo_near(up, down, buf):
+        @pl.when(lower)
+        def _():
+            arrive_low(up, buf)
+
+        @pl.when(jnp.logical_not(lower))
+        def _():
+            arrive_high(down, buf)
+
+    def halo_far(up, down, buf):
+        @pl.when(lower)
+        def _():
+            arrive_high(down, buf)
+
+        @pl.when(jnp.logical_not(lower))
+        def _():
+            arrive_low(up, buf)
 
     def halo_sent(up, down):
         @pl.when(me < n - 1)
@@ -134,23 +156,32 @@
 
     def fill(target, buf, a):
         own, edge = windows(buf[a], height, pairs)
-        target[:, 256 * a : 256 * a + 128] = own
-        target[:, 256 * a + 128 : 256 * (a + 1)] = edge
+        start = a * 256 if isinstance(a, int) else pl.multiple_of(a * 256, 256)
+        target[:, pl.ds(start, 256)] = jnp.concatenate([own, edge], axis=1)
 
     def plane_fwd(a):
+        start = a * 256 if isinstance(a, int) else pl.multiple_of(a * 256, 256)
         return lax.dot_general(
-            win[:, 256 * a : 256 * (a + 1)], wfwd[:, 256 * a : 256 * (a + 1)],
+            win[:, pl.ds(start, 256)], wfwd[:, pl.ds(start, 256)],
             (((1,), (1,)), ((), ())), preferred_element_type=F32,
+        )
+
+    def plane_bwd(a):
+        start = a * 256 if isinstance(a, int) else pl.multiple_of(a * 256, 256)
+        return jnp.dot(
+            dwin[:, pl.ds(start, 256)], wbwd[pl.ds(start, 256), :], preferred_element_type=F32
         )
 
     load_v.wait()
     fill(win, vbuf, 1)
     parts = plane_fwd(1)
     load_g.wait()
-    halo_arrive(v_up, v_down, vbuf)
-    fill(win, vbuf, 0)
-    fill(win, vbuf, 2)
-    parts = parts + plane_fwd(0) + plane_fwd(2)
+    halo_near(v_up, v_down, vbuf)
+    fill(win, vbuf, near)
+    parts = parts + plane_fwd(near)
+    halo_far(v_up, v_down, vbuf)
+    fill(win, vbuf, 2 - near)
+    parts = parts + plane_fwd(2 - near)
     pre = y_sum(parts, height)
     sig = 1.0 / (1.0 + jnp.exp(-pre))
     cot = pair_rows(gbuf[...], height, pairs).astype(F32)
@@ -243,14 +274,6 @@
             copies.append(copy)
         first_copies.append(copies)
 
-    halo_arrive(d_up, d_down, dbuf)
-    for a in range(3):
-        fill(dwin, dbuf, a)
-    back = jnp.dot(dwin[...], wbwd[...], preferred_element_type=F32)
-    grad = y_sum(back, height).astype(BF16)
-    for k in range(pairs):
-        ig_ref[0, 0, :, 128 * k : 128 * (k + 1)] = grad[height * k : height * (k + 1)]
-
     second_copies = []
     for k in range(1, mz):
         second_copies.append(pltpu.make_async_remote_copy(
@@ -270,6 +293,18 @@
             @pl.when((target < early) if stage == 0 else (target >= early))
             def _(copy=second_copies[k - 1]):
                 copy.start()
+
+    fill(dwin, dbuf, 1)
+    back = plane_bwd(1)
+    halo_near(d_up, d_down, dbuf)
+    fill(dwin, dbuf, near)
+    back = back + plane_bwd(near)
+    halo_far(d_up, d_down, dbuf)
+    fill(dwin, dbuf, 2 - near)
+    back = back + plane_bwd(2 - near)
+    grad = y_sum(back, height).astype(BF16)
+    for k in range(pairs):
+        ig_ref[0, 0, :, 128 * k : 128 * (k + 1)] = grad[height * k : height * (k + 1)]
 
     halo_sent(v_up, v_down)
     halo_sent(d_up, d_down)

time: 20.9 us -> 20.8 us (level)
  no operation moved by 1% of the time
where the time goes in v1:
time: 20.8 us; the launch traced here: 20.6 us
  Pallas kernels  20 us (96%)
  between operations  0.64 us (3%)
    pallas_call x1, Pallas kernels, per_device(): pl.pallas_call(functools.partial(kernel, geom), out_shape=(vmem(volume.sh...  19.3 us
    pallas_call x1, Pallas kernels, per_device(): pl.pallas_call(place, out_shape=tuple((jax.ShapeDtypeStruct(r.shape, r.dt...  0.68 us

profile of v1, /device:TPU:0, one launch (start us, length us, event | category | flops | bytes accessed | tf_op | source)
XLA Modules:
  0.0 20.6 jit_solution(11644945499625857586)
XLA Ops:
  0.6 19.3 %shard_map.58 = (bf16[1,1,16,2048]{3,2,1,0:T(8,128)(2,1)S(1)}, bf16[1,1,16,2048]{3,2,1,0:T(8,128)(2,1)S(1)}, f32[16,216]{1,0:T(8,128)S(1)}) custom-call(bf16[1,1,16,2048]{3,2,1,0:T(8,128)(2,1)} %v_ref.1, bf16[64,1728]{1,0:T(8,128)(2,1)} %bitcast.2, bf16[1,1,16,2048]{3,2,1,0:T(8,128)(2,1)} %g_ref.1), custom_call_target="tpu_custom_call" | custom-call | tf_op jit(solution)/shard_map/pallas_call | solution.py:352
  19.9 0.7 %shard_map.59 = (bf16[1,1,16,2048]{3,2,1,0:T(8,128)(2,1)}, bf16[1,1,16,2048]{3,2,1,0:T(8,128)(2,1)}, f32[16,216]{1,0:T(8,128)}) custom-call(bf16[1,1,16,2048]{3,2,1,0:T(8,128)(2,1)S(1)} %get-tuple-element.9.a_ref, bf16[1,1,16,2048]{3,2,1,0:T(8,128)(2,1)S(1)} %get-tuple-element.10.i_ref, f32[16,216]{1,0:T(8,128)S(1)} %get-tuple-element.11.w_ref), custom_call_target="tpu_custom_call" | custom-call | tf_op jit(solution)/shard_map/pallas_call | solution.py:384

commit v2 on v0

--- a/solution.py
+++ b/solution.py
@@ -21,11 +21,17 @@
     return jnp.concatenate([plane[:, 128 * k : 128 * (k + 1)] for k in range(pairs)], axis=0)
 
 
-def windows(plane, height, pairs):
-    own = pair_rows(plane, height, pairs)
-    zero = jnp.zeros((height, 128), own.dtype)
-    after = jnp.concatenate([own[height:], zero], axis=0)
-    before = jnp.concatenate([zero, own[:-height]], axis=0)
+def windows(buf, a, height, low, high):
+    zero = jnp.zeros((height, 128), buf.dtype)
+    count = buf.shape[2] // 128
+
+    def column(k):
+        return buf[a, :, 128 * k : 128 * (k + 1)] if 0 <= k < count else zero
+
+    own, after, before = (
+        jnp.concatenate([column(k + shift) for k in range(low, high)], axis=0)
+        for shift in (0, 1, -1)
+    )
     lane = lax.broadcasted_iota(jnp.int32, own.shape, 1)
     return own, jnp.where(lane < 64, after, before)
 
@@ -66,13 +72,15 @@
     load_g.start()
     pl.semaphore_wait(barrier, n + mz - 1)
 
-    def halo(source, buf, ssem, rsem):
+    def halo(source, buf, ssem, rsem, piece, low, high):
         up = pltpu.make_async_remote_copy(
-            src_ref=source, dst_ref=buf.at[0], send_sem=ssem.at[0], recv_sem=rsem.at[0],
+            src_ref=source.at[:, low:high], dst_ref=buf.at[0, :, low:high],
+            send_sem=ssem.at[piece, 0], recv_sem=rsem.at[piece, 0],
             device_id={"dp": lax.rem(me + 1, n)}, device_id_type=MESH,
         )
         down = pltpu.make_async_remote_copy(
-            src_ref=source, dst_ref=buf.at[2], send_sem=ssem.at[1], recv_sem=rsem.at[1],
+            src_ref=source.at[:, low:high], dst_ref=buf.at[2, :, low:high],
+            send_sem=ssem.at[piece, 1], recv_sem=rsem.at[piece, 1],
             device_id={"dp": lax.rem(me + n - 1, n)}, device_id_type=MESH,
         )
 
@@ -84,16 +92,16 @@
         def _():
             down.start()
 
-        return up, down
-
-    def halo_arrive(up, down, buf):
+        return up, down, buf, low, high
+
+    def halo_arrive(up, down, buf, low, high):
         @pl.when(me > 0)
         def _():
             up.wait_recv()
 
         @pl.when(me == 0)
         def _():
-            buf[0] = jnp.zeros(buf.shape[1:], buf.dtype)
+            buf[0, :, low:high] = jnp.zeros((height, high - low), buf.dtype)
 
         @pl.when(me < n - 1)
         def _():
@@ -101,9 +109,9 @@
 
         @pl.when(me == n - 1)
         def _():
-            buf[2] = jnp.zeros(buf.shape[1:], buf.dtype)
-
-    def halo_sent(up, down):
+            buf[2, :, low:high] = jnp.zeros((height, high - low), buf.dtype)
+
+    def halo_sent(up, down, *_):
         @pl.when(me < n - 1)
         def _():
             up.wait_send()
@@ -112,7 +120,12 @@
         def _():
             down.wait_send()
 
-    v_up, v_down = halo(v_ref.at[0, 0], vbuf, vsend, vrecv)
+    half = pairs // 2
+    cut = 128 * (half + 1)
+    v_halos = [
+        halo(v_ref.at[0, 0], vbuf, vsend, vrecv, piece, low, high)
+        for piece, (low, high) in enumerate(((0, cut), (cut, 128 * pairs)))
+    ]
 
     load_w.wait()
     zero = jnp.zeros((64, 64), BF16)
@@ -132,33 +145,45 @@
                 [left, right], axis=1
             )
 
-    def fill(target, buf, a):
-        own, edge = windows(buf[a], height, pairs)
-        target[:, 256 * a : 256 * a + 128] = own
-        target[:, 256 * a + 128 : 256 * (a + 1)] = edge
-
-    def plane_fwd(a):
+    def fill(target, buf, a, low, high):
+        own, edge = windows(buf, a, height, low, high)
+        target[height * low : height * high, 256 * a : 256 * a + 128] = own
+        target[height * low : height * high, 256 * a + 128 : 256 * (a + 1)] = edge
+
+    def plane_fwd(a, rows):
         return lax.dot_general(
-            win[:, 256 * a : 256 * (a + 1)], wfwd[:, 256 * a : 256 * (a + 1)],
+            win[rows, 256 * a : 256 * (a + 1)], wfwd[:, 256 * a : 256 * (a + 1)],
             (((1,), (1,)), ((), ())), preferred_element_type=F32,
         )
 
     load_v.wait()
-    fill(win, vbuf, 1)
-    parts = plane_fwd(1)
+    fill(win, vbuf, 1, 0, pairs)
+    halves = ((0, half), (half, pairs))
+    middle = [plane_fwd(1, slice(height * low, height * high)) for low, high in halves]
     load_g.wait()
-    halo_arrive(v_up, v_down, vbuf)
-    fill(win, vbuf, 0)
-    fill(win, vbuf, 2)
-    parts = parts + plane_fwd(0) + plane_fwd(2)
-    pre = y_sum(parts, height)
-    sig = 1.0 / (1.0 + jnp.exp(-pre))
-    cot = pair_rows(gbuf[...], height, pairs).astype(F32)
-    delta = (cot * sig * (1.0 + pre * (1.0 - sig))).astype(BF16)
-    for k in range(pairs):
-        dbuf[1, :, 128 * k : 128 * (k + 1)] = delta[height * k : height * (k + 1)]
-
-    d_up, d_down = halo(dbuf.at[1], dbuf, dsend, drecv)
+    deltas, d_halos = [], []
+    for piece, (low, high) in enumerate(halves):
+        rows = slice(height * low, height * high)
+        halo_arrive(*v_halos[piece])
+        fill(win, vbuf, 0, low, high)
+        fill(win, vbuf, 2, low, high)
+        parts = middle[piece] + plane_fwd(0, rows) + plane_fwd(2, rows)
+        pre = y_sum(parts, height)
+        sig = 1.0 / (1.0 + jnp.exp(-pre))
+        cot = pair_rows(gbuf[:, 128 * low : 128 * high], height, high - low).astype(F32)
+        delta = (cot * sig * (1.0 + pre * (1.0 - sig))).astype(BF16)
+        for k in range(low, high):
+            at = slice(height * (k - low), height * (k - low + 1))
+            dbuf[1, :, 128 * k : 128 * (k + 1)] = delta[at]
+        d_halos.append(
+            halo(dbuf.at[1], dbuf, dsend, drecv, piece, 128 * low, 128 * high)
+        )
+        act = (pre * sig).astype(BF16)
+        for k in range(low, high):
+            at = slice(height * (k - low), height * (k - low + 1))
+            act_ref[0, 0, :, 128 * k : 128 * (k + 1)] = act[at]
+        deltas.append(delta)
+    delta = jnp.concatenate(deltas, axis=0)
 
     wide_delta = delta.astype(F32)
     row = lax.broadcasted_iota(jnp.int32, wide_delta.shape, 0) % height
@@ -222,10 +247,6 @@
     weight_terms((0, 1), 0, early, 0)
     weight_terms((2,), early, mz, 1)
 
-    act = (pre * sig).astype(BF16)
-    for k in range(pairs):
-        act_ref[0, 0, :, 128 * k : 128 * (k + 1)] = act[height * k : height * (k + 1)]
-
     first_copies = []
     for stage, (low_z, high_z) in enumerate(parts_z):
         zero_copies[stage].wait_recv()
@@ -243,14 +264,6 @@
             copies.append(copy)
         first_copies.append(copies)
 
-    halo_arrive(d_up, d_down, dbuf)
-    for a in range(3):
-        fill(dwin, dbuf, a)
-    back = jnp.dot(dwin[...], wbwd[...], preferred_element_type=F32)
-    grad = y_sum(back, height).astype(BF16)
-    for k in range(pairs):
-        ig_ref[0, 0, :, 128 * k : 128 * (k + 1)] = grad[height * k : height * (k + 1)]
-
     second_copies = []
     for k in range(1, mz):
         second_copies.append(pltpu.make_async_remote_copy(
@@ -271,8 +284,17 @@
             def _(copy=second_copies[k - 1]):
                 copy.start()
 
-    halo_sent(v_up, v_down)
-    halo_sent(d_up, d_down)
+    for piece in d_halos:
+        halo_arrive(*piece)
+    for a in range(3):
+        fill(dwin, dbuf, a, 0, pairs)
+    back = jnp.dot(dwin[...], wbwd[...], preferred_element_type=F32)
+    grad = y_sum(back, height).astype(BF16)
+    for k in range(pairs):
+        ig_ref[0, 0, :, 128 * k : 128 * (k + 1)] = grad[height * k : height * (k + 1)]
+
+    for piece in v_halos + d_halos:
+        halo_sent(*piece)
     for copy in zero_copies + first_copies[0] + first_copies[1]:
         copy.wait_send()
     total = sum1[z].astype(F32)
@@ -338,7 +360,7 @@
             vmem((n - 1, m // 2, wide, padded, 128), BF16),
             vmem((m // 2, wide, padded, 128), BF16),
             vmem((m // 2 - 1, wide, padded, 128), BF16),
-            dma((3,)), dma((2,)), dma((2,)), dma((2,)), dma((2,)),
+            dma((3,)), dma((2, 2)), dma((2, 2)), dma((2, 2)), dma((2, 2)),
             dma((2,)), dma((2,)), dma((2, n - 1)), dma((2, n - 1)),
             dma((m // 2 - 1,)), dma((m // 2 - 1,)),
         ],

time: 20.9 us -> 19.9 us (0.952)
  Pallas kernels: 20.1 us -> 19.1 us
    pallas_call x1, Pallas kernels: 19.4 us -> 18.4 us  [per_device(): pl.pallas_call(functools.partial(kernel, geom), out_shape=(vmem(volume.sh...]
where the time goes in v2:
time: 19.9 us; the launch traced here: 19.8 us
  Pallas kernels  19.1 us (96%)
  between operations  0.64 us (3%)
    pallas_call x1, Pallas kernels, per_device(): pl.pallas_call(functools.partial(kernel, geom), out_shape=(vmem(volume.sh...  18.4 us
    pallas_call x1, Pallas kernels, per_device(): pl.pallas_call(place, out_shape=tuple((jax.ShapeDtypeStruct(r.shape, r.dt...  0.68 us

profile of v2, /device:TPU:0, one launch (start us, length us, event | category | flops | bytes accessed | tf_op | source)
XLA Modules:
  0.0 19.8 jit_solution(12663578340461630031)
XLA Ops:
  0.6 18.4 %shard_map.58 = (bf16[1,1,16,2048]{3,2,1,0:T(8,128)(2,1)S(1)}, bf16[1,1,16,2048]{3,2,1,0:T(8,128)(2,1)S(1)}, f32[16,216]{1,0:T(8,128)S(1)}) custom-call(bf16[1,1,16,2048]{3,2,1,0:T(8,128)(2,1)} %v_ref.1, bf16[64,1728]{1,0:T(8,128)(2,1)} %bitcast.2, bf16[1,1,16,2048]{3,2,1,0:T(8,128)(2,1)} %g_ref.1), custom_call_target="tpu_custom_call" | custom-call | tf_op jit(solution)/shard_map/pallas_call | solution.py:339
  19.1 0.7 %shard_map.59 = (bf16[1,1,16,2048]{3,2,1,0:T(8,128)(2,1)}, bf16[1,1,16,2048]{3,2,1,0:T(8,128)(2,1)}, f32[16,216]{1,0:T(8,128)}) custom-call(bf16[1,1,16,2048]{3,2,1,0:T(8,128)(2,1)S(1)} %get-tuple-element.9.a_ref, bf16[1,1,16,2048]{3,2,1,0:T(8,128)(2,1)S(1)} %get-tuple-element.10.i_ref, f32[16,216]{1,0:T(8,128)S(1)} %get-tuple-element.11.w_ref), custom_call_target="tpu_custom_call" | custom-call | tf_op jit(solution)/shard_map/pallas_call | solution.py:371

commit v3 on v2

--- a/solution.py
+++ b/solution.py
@@ -138,12 +138,6 @@
             wfwd[128 * b : 128 * (b + 1), 256 * a : 256 * (a + 1)] = jnp.concatenate(
                 [top, bottom], axis=0
             )
-            left = jnp.concatenate([k1, k0, zero, k2], axis=0)
-            right = jnp.concatenate([k2, k1, k0, zero], axis=0)
-            fa, fb = 2 - a, 2 - b
-            wbwd[256 * fa : 256 * (fa + 1), 128 * fb : 128 * (fb + 1)] = jnp.concatenate(
-                [left, right], axis=1
-            )
 
     def fill(target, buf, a, low, high):
         own, edge = windows(buf, a, height, low, high)
@@ -161,7 +155,7 @@
     halves = ((0, half), (half, pairs))
     middle = [plane_fwd(1, slice(height * low, height * high)) for low, high in halves]
     load_g.wait()
-    deltas, d_halos = [], []
+    deltas, d_halos, acts = [], [], []
     for piece, (low, high) in enumerate(halves):
         rows = slice(height * low, height * high)
         halo_arrive(*v_halos[piece])
@@ -178,10 +172,7 @@
         d_halos.append(
             halo(dbuf.at[1], dbuf, dsend, drecv, piece, 128 * low, 128 * high)
         )
-        act = (pre * sig).astype(BF16)
-        for k in range(low, high):
-            at = slice(height * (k - low), height * (k - low + 1))
-            act_ref[0, 0, :, 128 * k : 128 * (k + 1)] = act[at]
+        acts.append((pre * sig).astype(BF16))
         deltas.append(delta)
     delta = jnp.concatenate(deltas, axis=0)
 
@@ -247,6 +238,20 @@
     weight_terms((0, 1), 0, early, 0)
     weight_terms((2,), early, mz, 1)
 
+    for (low, high), act in zip(halves, acts):
+        for k in range(low, high):
+            at = slice(height * (k - low), height * (k - low + 1))
+            act_ref[0, 0, :, 128 * k : 128 * (k + 1)] = act[at]
+    for a in range(3):
+        for b in range(3):
+            base = (a * 9 + b * 3) * 64
+            k0, k1, k2 = (wbuf[:, base + 64 * c : base + 64 * (c + 1)] for c in range(3))
+            left = jnp.concatenate([k1, k0, zero, k2], axis=0)
+            right = jnp.concatenate([k2, k1, k0, zero], axis=0)
+            fa, fb = 2 - a, 2 - b
+            wbwd[256 * fa : 256 * (fa + 1), 128 * fb : 128 * (fb + 1)] = jnp.concatenate(
+                [left, right], axis=1
+            )
     first_copies = []
     for stage, (low_z, high_z) in enumerate(parts_z):
         zero_copies[stage].wait_recv()
@@ -264,6 +269,8 @@
             copies.append(copy)
         first_copies.append(copies)
 
+    fill(dwin, dbuf, 1, 0, pairs)
+    back = jnp.dot(dwin[:, 256:512], wbwd[256:512, :], preferred_element_type=F32)
     second_copies = []
     for k in range(1, mz):
         second_copies.append(pltpu.make_async_remote_copy(
@@ -286,9 +293,12 @@
 
     for piece in d_halos:
         halo_arrive(*piece)
-    for a in range(3):
+    for a in (0, 2):
         fill(dwin, dbuf, a, 0, pairs)
-    back = jnp.dot(dwin[...], wbwd[...], preferred_element_type=F32)
+        back = back + jnp.dot(
+            dwin[:, 256 * a : 256 * (a + 1)], wbwd[256 * a : 256 * (a + 1), :],
+            preferred_element_type=F32,
+        )
     grad = y_sum(back, height).astype(BF16)
     for k in range(pairs):
         ig_ref[0, 0, :, 128 * k : 128 * (k + 1)] = grad[height * k : height * (k + 1)]

time: 19.9 us -> 20.3 us (1.020)
  Pallas kernels: 19.1 us -> 19.5 us
    pallas_call x1, Pallas kernels: 18.4 us -> 18.8 us  [per_device(): pl.pallas_call(functools.partial(kernel, geom), out_shape=(vmem(volume.sh...]
where the time goes in v3:
time: 20.3 us; the launch traced here: 20.2 us
  Pallas kernels  19.5 us (96%)
  between operations  0.64 us (3%)
    pallas_call x1, Pallas kernels, per_device(): pl.pallas_call(functools.partial(kernel, geom), out_shape=(vmem(volume.sh...  18.8 us
    pallas_call x1, Pallas kernels, per_device(): pl.pallas_call(place, out_shape=tuple((jax.ShapeDtypeStruct(r.shape, r.dt...  0.68 us

profile of v3, /device:TPU:0, one launch (start us, length us, event | category | flops | bytes accessed | tf_op | source)
XLA Modules:
  0.0 20.2 jit_solution(3474123541326278292)
XLA Ops:
  0.6 18.8 %shard_map.58 = (bf16[1,1,16,2048]{3,2,1,0:T(8,128)(2,1)S(1)}, bf16[1,1,16,2048]{3,2,1,0:T(8,128)(2,1)S(1)}, f32[16,216]{1,0:T(8,128)S(1)}) custom-call(bf16[1,1,16,2048]{3,2,1,0:T(8,128)(2,1)} %v_ref.1, bf16[64,1728]{1,0:T(8,128)(2,1)} %bitcast.2, bf16[1,1,16,2048]{3,2,1,0:T(8,128)(2,1)} %g_ref.1), custom_call_target="tpu_custom_call" | custom-call | tf_op jit(solution)/shard_map/pallas_call | solution.py:349
  19.5 0.7 %shard_map.59 = (bf16[1,1,16,2048]{3,2,1,0:T(8,128)(2,1)}, bf16[1,1,16,2048]{3,2,1,0:T(8,128)(2,1)}, f32[16,216]{1,0:T(8,128)}) custom-call(bf16[1,1,16,2048]{3,2,1,0:T(8,128)(2,1)S(1)} %get-tuple-element.9.a_ref, bf16[1,1,16,2048]{3,2,1,0:T(8,128)(2,1)S(1)} %get-tuple-element.10.i_ref, f32[16,216]{1,0:T(8,128)S(1)} %get-tuple-element.11.w_ref), custom_call_target="tpu_custom_call" | custom-call | tf_op jit(solution)/shard_map/pallas_call | solution.py:381

commit v4 on v2

--- a/solution.py
+++ b/solution.py
@@ -138,6 +138,11 @@
             wfwd[128 * b : 128 * (b + 1), 256 * a : 256 * (a + 1)] = jnp.concatenate(
                 [top, bottom], axis=0
             )
+
+    for a in range(3):
+        for b in range(3):
+            base = (a * 9 + b * 3) * 64
+            k0, k1, k2 = (wbuf[:, base + 64 * c : base + 64 * (c + 1)] for c in range(3))
             left = jnp.concatenate([k1, k0, zero, k2], axis=0)
             right = jnp.concatenate([k2, k1, k0, zero], axis=0)
             fa, fb = 2 - a, 2 - b
@@ -161,7 +166,7 @@
     halves = ((0, half), (half, pairs))
     middle = [plane_fwd(1, slice(height * low, height * high)) for low, high in halves]
     load_g.wait()
-    deltas, d_halos = [], []
+    deltas, d_halos, acts = [], [], []
     for piece, (low, high) in enumerate(halves):
         rows = slice(height * low, height * high)
         halo_arrive(*v_halos[piece])
@@ -178,10 +183,7 @@
         d_halos.append(
             halo(dbuf.at[1], dbuf, dsend, drecv, piece, 128 * low, 128 * high)
         )
-        act = (pre * sig).astype(BF16)
-        for k in range(low, high):
-            at = slice(height * (k - low), height * (k - low + 1))
-            act_ref[0, 0, :, 128 * k : 128 * (k + 1)] = act[at]
+        acts.append((pre * sig).astype(BF16))
         deltas.append(delta)
     delta = jnp.concatenate(deltas, axis=0)
 
@@ -264,6 +266,12 @@
             copies.append(copy)
         first_copies.append(copies)
 
+    for (low, high), act in zip(halves, acts):
+        for k in range(low, high):
+            at = slice(height * (k - low), height * (k - low + 1))
+            act_ref[0, 0, :, 128 * k : 128 * (k + 1)] = act[at]
+    fill(dwin, dbuf, 1, 0, pairs)
+    back = jnp.dot(dwin[:, 256:512], wbwd[256:512, :], preferred_element_type=F32)
     second_copies = []
     for k in range(1, mz):
         second_copies.append(pltpu.make_async_remote_copy(
@@ -286,9 +294,12 @@
 
     for piece in d_halos:
         halo_arrive(*piece)
-    for a in range(3):
+    for a in (0, 2):
         fill(dwin, dbuf, a, 0, pairs)
-    back = jnp.dot(dwin[...], wbwd[...], preferred_element_type=F32)
+        back = back + jnp.dot(
+            dwin[:, 256 * a : 256 * (a + 1)], wbwd[256 * a : 256 * (a + 1), :],
+            preferred_element_type=F32,
+        )
     grad = y_sum(back, height).astype(BF16)
     for k in range(pairs):
         ig_ref[0, 0, :, 128 * k : 128 * (k + 1)] = grad[height * k : height * (k + 1)]

time: 19.9 us -> 19.9 us (level)
  no operation moved by 1% of the time
where the time goes in v4:
time: 19.9 us; the launch traced here: 19.8 us
  Pallas kernels  19.1 us (96%)
  between operations  0.64 us (3%)
    pallas_call x1, Pallas kernels, per_device(): pl.pallas_call(functools.partial(kernel, geom), out_shape=(vmem(volume.sh...  18.4 us
    pallas_call x1, Pallas kernels, per_device(): pl.pallas_call(place, out_shape=tuple((jax.ShapeDtypeStruct(r.shape, r.dt...  0.68 us

profile of v4, /device:TPU:0, one launch (start us, length us, event | category | flops | bytes accessed | tf_op | source)
XLA Modules:
  0.0 19.8 jit_solution(17803916895696768151)
XLA Ops:
  0.6 18.4 %shard_map.58 = (bf16[1,1,16,2048]{3,2,1,0:T(8,128)(2,1)S(1)}, bf16[1,1,16,2048]{3,2,1,0:T(8,128)(2,1)S(1)}, f32[16,216]{1,0:T(8,128)S(1)}) custom-call(bf16[1,1,16,2048]{3,2,1,0:T(8,128)(2,1)} %v_ref.1, bf16[64,1728]{1,0:T(8,128)(2,1)} %bitcast.2, bf16[1,1,16,2048]{3,2,1,0:T(8,128)(2,1)} %g_ref.1), custom_call_target="tpu_custom_call" | custom-call | tf_op jit(solution)/shard_map/pallas_call | solution.py:350
  19.1 0.7 %shard_map.59 = (bf16[1,1,16,2048]{3,2,1,0:T(8,128)(2,1)}, bf16[1,1,16,2048]{3,2,1,0:T(8,128)(2,1)}, f32[16,216]{1,0:T(8,128)}) custom-call(bf16[1,1,16,2048]{3,2,1,0:T(8,128)(2,1)S(1)} %get-tuple-element.9.a_ref, bf16[1,1,16,2048]{3,2,1,0:T(8,128)(2,1)S(1)} %get-tuple-element.10.i_ref, f32[16,216]{1,0:T(8,128)S(1)} %get-tuple-element.11.w_ref), custom_call_target="tpu_custom_call" | custom-call | tf_op jit(solution)/shard_map/pallas_call | solution.py:382

commit v5 on v4

--- a/solution.py
+++ b/solution.py
@@ -166,7 +166,14 @@
     halves = ((0, half), (half, pairs))
     middle = [plane_fwd(1, slice(height * low, height * high)) for low, high in halves]
     load_g.wait()
-    deltas, d_halos, acts = [], [], []
+    d_halos, acts = [], []
+    spans = (slice(0, 512), slice(512, 768))
+
+    def products(left, rows, span):
+        return lax.dot_general(
+            left, win[rows, span], (((0,), (0,)), ((), ())), preferred_element_type=F32
+        )
+
     for piece, (low, high) in enumerate(halves):
         rows = slice(height * low, height * high)
         halo_arrive(*v_halos[piece])
@@ -184,14 +191,14 @@
             halo(dbuf.at[1], dbuf, dsend, drecv, piece, 128 * low, 128 * high)
         )
         acts.append((pre * sig).astype(BF16))
-        deltas.append(delta)
-    delta = jnp.concatenate(deltas, axis=0)
-
-    wide_delta = delta.astype(F32)
-    row = lax.broadcasted_iota(jnp.int32, wide_delta.shape, 0) % height
-    ahead = jnp.where(row == height - 1, 0.0, rolled(wide_delta, -1, 0)).astype(BF16)
-    behind = jnp.where(row == 0, 0.0, rolled(wide_delta, 1, 0)).astype(BF16)
-    moved = jnp.concatenate([ahead, delta, behind], axis=1)
+        wide_delta = delta.astype(F32)
+        row = lax.broadcasted_iota(jnp.int32, wide_delta.shape, 0) % height
+        ahead = jnp.where(row == height - 1, 0.0, rolled(wide_delta, -1, 0)).astype(BF16)
+        behind = jnp.where(row == 0, 0.0, rolled(wide_delta, 1, 0)).astype(BF16)
+        moved = jnp.concatenate([ahead, delta, behind], axis=1)
+        if piece == 0:
+            first_terms = [products(moved, rows, span) for span in spans]
+
     lane = lax.broadcasted_iota(jnp.int32, (64, 128), 1) < 64
     early = sum(2 * (q + 1) * rows_out <= 9 * 128 for q in range(mz))
     parts_z = ((0, early), (early, mz))
@@ -200,10 +207,7 @@
     lanes = lax.broadcasted_iota(jnp.int32, (64, 128), 1)
 
     def weight_terms(planes, low_z, high_z, stage):
-        span = win[:, 256 * planes[0] : 256 * (planes[-1] + 1)]
-        terms = lax.dot_general(
-            moved, span, (((0,), (0,)), ((), ())), preferred_element_type=F32
-        )
+        terms = first_terms[stage] + products(moved, rows, spans[stage])
         quads = []
         for p in range(len(planes)):
             for b in range(3):

time: 19.9 us -> 20.3 us (1.020)
  Pallas kernels: 19.1 us -> 19.5 us
    pallas_call x1, Pallas kernels: 18.4 us -> 18.8 us  [per_device(): pl.pallas_call(functools.partial(kernel, geom), out_shape=(vmem(volume.sh...]
where the time goes in v5:
time: 20.3 us; the launch traced here: 20.1 us
  Pallas kernels  19.5 us (96%)
  between operations  0.64 us (3%)
    pallas_call x1, Pallas kernels, per_device(): pl.pallas_call(functools.partial(kernel, geom), out_shape=(vmem(volume.sh...  18.8 us
    pallas_call x1, Pallas kernels, per_device(): pl.pallas_call(place, out_shape=tuple((jax.ShapeDtypeStruct(r.shape, r.dt...  0.68 us

profile of v5, /device:TPU:0, one launch (start us, length us, event | category | flops | bytes accessed | tf_op | source)
XLA Modules:
  0.0 20.1 jit_solution(14579015320369589175)
XLA Ops:
  0.6 18.8 %shard_map.58 = (bf16[1,1,16,2048]{3,2,1,0:T(8,128)(2,1)S(1)}, bf16[1,1,16,2048]{3,2,1,0:T(8,128)(2,1)S(1)}, f32[16,216]{1,0:T(8,128)S(1)}) custom-call(bf16[1,1,16,2048]{3,2,1,0:T(8,128)(2,1)} %v_ref.1, bf16[64,1728]{1,0:T(8,128)(2,1)} %bitcast.2, bf16[1,1,16,2048]{3,2,1,0:T(8,128)(2,1)} %g_ref.1), custom_call_target="tpu_custom_call" | custom-call | tf_op jit(solution)/shard_map/pallas_call | solution.py:354
  19.4 0.7 %shard_map.59 = (bf16[1,1,16,2048]{3,2,1,0:T(8,128)(2,1)}, bf16[1,1,16,2048]{3,2,1,0:T(8,128)(2,1)}, f32[16,216]{1,0:T(8,128)}) custom-call(bf16[1,1,16,2048]{3,2,1,0:T(8,128)(2,1)S(1)} %get-tuple-element.9.a_ref, bf16[1,1,16,2048]{3,2,1,0:T(8,128)(2,1)S(1)} %get-tuple-element.10.i_ref, f32[16,216]{1,0:T(8,128)S(1)} %get-tuple-element.11.w_ref), custom_call_target="tpu_custom_call" | custom-call | tf_op jit(solution)/shard_map/pallas_call | solution.py:386

commit v6 on v4

--- a/solution.py
+++ b/solution.py
@@ -193,8 +193,8 @@
     behind = jnp.where(row == 0, 0.0, rolled(wide_delta, 1, 0)).astype(BF16)
     moved = jnp.concatenate([ahead, delta, behind], axis=1)
     lane = lax.broadcasted_iota(jnp.int32, (64, 128), 1) < 64
-    early = sum(2 * (q + 1) * rows_out <= 9 * 128 for q in range(mz))
-    parts_z = ((0, early), (early, mz))
+    early = mz
+    parts_z = ((0, mz),)
     zero_copies = []
     gathered = []
     lanes = lax.broadcasted_iota(jnp.int32, (64, 128), 1)
@@ -246,8 +246,7 @@
         copy.start()
         zero_copies.append(copy)
 
-    weight_terms((0, 1), 0, early, 0)
-    weight_terms((2,), early, mz, 1)
+    weight_terms((0, 1, 2), 0, mz, 0)
 
     first_copies = []
     for stage, (low_z, high_z) in enumerate(parts_z):
@@ -306,7 +305,7 @@
 
     for piece in v_halos + d_halos:
         halo_sent(*piece)
-    for copy in zero_copies + first_copies[0] + first_copies[1]:
+    for copy in zero_copies + first_copies[0]:
         copy.wait_send()
     total = sum1[z].astype(F32)
     for k in range(1, mz):

time: 19.9 us -> 20 us (level)
  no operation moved by 1% of the time
where the time goes in v6:
time: 20 us; the launch traced here: 19.9 us
  Pallas kernels  19.2 us (96%)
  between operations  0.64 us (3%)
    pallas_call x1, Pallas kernels, per_device(): pl.pallas_call(functools.partial(kernel, geom), out_shape=(vmem(volume.sh...  18.5 us
    pallas_call x1, Pallas kernels, per_device(): pl.pallas_call(place, out_shape=tuple((jax.ShapeDtypeStruct(r.shape, r.dt...  0.68 us

profile of v6, /device:TPU:0, one launch (start us, length us, event | category | flops | bytes accessed | tf_op | source)
XLA Modules:
  0.0 19.9 jit_solution(17364580166806651893)
XLA Ops:
  0.6 18.5 %shard_map.58 = (bf16[1,1,16,2048]{3,2,1,0:T(8,128)(2,1)S(1)}, bf16[1,1,16,2048]{3,2,1,0:T(8,128)(2,1)S(1)}, f32[16,216]{1,0:T(8,128)S(1)}) custom-call(bf16[1,1,16,2048]{3,2,1,0:T(8,128)(2,1)} %v_ref.1, bf16[64,1728]{1,0:T(8,128)(2,1)} %bitcast.2, bf16[1,1,16,2048]{3,2,1,0:T(8,128)(2,1)} %g_ref.1), custom_call_target="tpu_custom_call" | custom-call | tf_op jit(solution)/shard_map/pallas_call | solution.py:349
  19.2 0.7 %shard_map.59 = (bf16[1,1,16,2048]{3,2,1,0:T(8,128)(2,1)}, bf16[1,1,16,2048]{3,2,1,0:T(8,128)(2,1)}, f32[16,216]{1,0:T(8,128)}) custom-call(bf16[1,1,16,2048]{3,2,1,0:T(8,128)(2,1)S(1)} %get-tuple-element.9.a_ref, bf16[1,1,16,2048]{3,2,1,0:T(8,128)(2,1)S(1)} %get-tuple-element.10.i_ref, f32[16,216]{1,0:T(8,128)S(1)} %get-tuple-element.11.w_ref), custom_call_target="tpu_custom_call" | custom-call | tf_op jit(solution)/shard_map/pallas_call | solution.py:381
